TPU v7x, 256 devices: a whole 4x4x8 slice. The times are simulated.
256 devices in a mesh: outer: 8 (over x, core), inner: 32 (over y, z).
Axes of the slice: x: 4, y: 4, z: 8, core: 2. Of those that a mesh axis runs over, the one named last changes fastest.
Arguments:
- basis: float32 [32768, 1024], P(('outer', 'inner')), may hold values from -0.1875 to 0.1875
- fields: float32 [32768, 64], P(('outer', 'inner')), may hold values from -6 to 6
- positions: int32 [32768], P(('outer', 'inner')), may hold values from 0 to 511
- nugget: float32 [32768], P(('outer', 'inner')), may hold values from 0.2 to 2
Outputs:
- posterior_mean: float32 [32768, 64], P(('outer', 'inner'))
- root_coef: float32 [512, 64], replicated
All inputs are finite; a program needn't handle non-finite values.
Results may differ from a plain program's by a relative error of at most 0.0001.
Values sent between devices are 32-bit elements; how exact they have to be, the bound alone decides.
A program may use at most 64 MiB of HBM per device.

v0:
```python
import jax
import jax.numpy as jnp
from jax import lax
from jax.sharding import Mesh
from jax.sharding import PartitionSpec as P

M = 512
R = 512
K = 1024
RANGE = 8
INNER = ("inner_0", "inner_1")
OUTER_INNER = ("outer", "inner_0", "inner_1")


def over_pieces(x, axis):
    return lax.all_gather(x, axis).sum(0)


def summed_rows(total, axes):
    for axis in axes:
        total = lax.psum_scatter(total, axis, scatter_dimension=0, tiled=True)
    return total


def sent_to_all(x, axis):
    copies = jnp.broadcast_to(x, (lax.axis_size(axis), *x.shape))
    return lax.all_to_all(copies, axis, split_axis=0, concat_axis=0, tiled=True)


def in_order(parts, dim):
    dims = list(parts.shape[1:])
    dims[dim] *= parts.shape[0]
    return jnp.moveaxis(parts, 0, dim).reshape(dims)


def collect(x, axis, dim):
    parts = sent_to_all(x, axis)
    return in_order(parts, dim)


def hdot(left, right):
    return jnp.dot(left, right, precision=lax.Precision.HIGHEST)


def lower_solve(factor, values):
    return lax.linalg.triangular_solve(factor, values, left_side=True, lower=True)


def factor_solve(factor, values):
    first = lax.linalg.triangular_solve(factor, values, left_side=True, lower=True)
    return lax.linalg.triangular_solve(factor, first, left_side=True, lower=True, transpose_a=True)


def shards(basis, fields, positions, nugget):
    group_size = lax.axis_size(INNER)
    region_share = M // group_size
    root_share = R // group_size
    block_rows = region_share + root_share
    leaf_rows = basis.shape[0]
    distance = jnp.abs(positions[:, None] - positions[None, :]).astype(jnp.float32)
    covariance = jnp.exp(-distance / RANGE) + jnp.diag(nugget)
    factor = jnp.linalg.cholesky(covariance)
    whitened = lower_solve(factor, jnp.concatenate([basis, fields], axis=1))
    white_basis = whitened[:, :K]
    white_fields = whitened[:, K:]
    rhs_sum = over_pieces(hdot(white_basis.T, white_fields), INNER)
    rhs_region = rhs_sum[:M]
    rhs_root = rhs_sum[M:]
    blocks = block_rows * lax.axis_size(INNER) // block_rows
    first_block = jnp.int32(0) // block_rows
    region = lax.dynamic_slice_in_dim(
        white_basis, first_block * region_share, blocks * region_share, 1
    )
    root_part = lax.dynamic_slice_in_dim(white_basis, M, blocks * root_share, 1)
    chosen = jnp.concatenate(
        [
            region.reshape(leaf_rows, blocks, region_share),
            root_part.reshape(leaf_rows, blocks, root_share),
        ],
        axis=2,
    )
    pieces = summed_rows(
        hdot(chosen.reshape(leaf_rows, block_rows * lax.axis_size(INNER)).T, white_basis), INNER
    )
    upper_rows = collect(pieces[:region_share], INNER, 0)
    root_rows = pieces[region_share:]
    knot_block = upper_rows[:, :M] + jnp.eye(M, dtype=jnp.float32)
    cross_block = upper_rows[:, M:]
    knot_factor = jnp.linalg.cholesky(knot_block)
    solved = factor_solve(knot_factor, jnp.concatenate([root_rows[:, :M].T, rhs_region], axis=1))
    schur_part = root_rows[:, M:] - hdot(solved[:, :root_share].T, cross_block)
    reduced = rhs_root - hdot(cross_block.T, solved[:, root_share:])
    schur_total, reduced_total = lax.psum((schur_part, reduced), "outer")
    device_index = lax.axis_index(INNER)
    wanted = device_index * root_share + jnp.arange(root_share, dtype=jnp.int32)
    identity_rows = (jnp.arange(R, dtype=jnp.int32)[None, :] == wanted[:, None]).astype(jnp.float32)
    precision_root = collect(identity_rows + schur_total, INNER, 0)
    root_coef = factor_solve(jnp.linalg.cholesky(precision_root), reduced_total)
    region_coef = factor_solve(knot_factor, rhs_region - hdot(cross_block, root_coef))
    posterior_mean = hdot(basis[:, :M], region_coef) + hdot(basis[:, M:], root_coef)
    return (posterior_mean, root_coef)


def solution(mesh):
    split = Mesh(mesh.devices.reshape(mesh.shape["outer"], 4, 8), ("outer", "inner_0", "inner_1"))
    in_specs = (P(OUTER_INNER, None), P(OUTER_INNER, None), P(OUTER_INNER), P(OUTER_INNER))
    out_specs = (P(OUTER_INNER, None), P())
    return jax.shard_map(
        shards, mesh=split, in_specs=in_specs, out_specs=out_specs, check_vma=False
    )
```

profile of v0, /device:TPU:32, one launch (start us, length us, event | category | flops | bytes accessed | tf_op | source)
XLA Modules:
  0.0 603.8 jit_solution(14743809966694893969)
XLA Ops:
  9.8 11.7 %cholesky.116 = f32[128,128]{1,0:T(8,128)S(1)} custom-call(f32[128,128]{1,0:T(8,128)S(1)} %fusion.115), custom_call_target="Cholesky" | custom-call | tf_op jit(solution)/shard_map/jit(cholesky)/cholesky | solution.py:62
  22.8 9.8 %custom-call.37 = f32[1,128,128]{1,2,0:T(8,128)S(1)} custom-call(f32[1,128,128]{2,1,0:T(8,128)S(1)} %fusion.85), custom_call_target="InvertDiagBlocksLowerTriangular" | custom-call | tf_op jit(solution)/shard_map/triangular_solve | solution.py:46
  32.6 2.1 fusion.6
  34.9 5.0 fusion.12
  39.9 52.1 %reduce-scatter.3.cloned.1.call-done = f32[256,1024]{1,0:T(8,128)} async-done(((f32[1024,1024]{1,0:T(8,128)}), f32[256,1024]{1,0:T(8,128)}) %reduce-scatter.3.cloned.1.call-update) | async-done | bytes 1048592 | tf_op jit(solution)/shard_map/reduce_scatter | solution.py:21
  92.1 1.4 fusion.10
  93.5 40.5 %reduce-scatter.5.cloned.1.call-done = f32[32,1024]{1,0:T(8,128)} async-done(((f32[256,1024]{1,0:T(8,128)}), f32[32,1024]{1,0:T(8,128)}) %reduce-scatter.5.cloned.1.call-update) | async-done | bytes 131088 | tf_op jit(solution)/shard_map/reduce_scatter | solution.py:21
  134.9 1.6 broadcast_in_dim.36
  136.5 8.5 %all-to-all-start = ((f32[32,16,1024]{2,1,0:T(8,128)}), f32[32,16,1024]{2,1,0:T(8,128)S(1)}, u32[]{:S(2)}, u32[]{:S(2)}) async-start(f32[32,16,1024]{2,1,0:T(8,128)} %broadcast_in_dim.36), calls=%async_computation.2 | async-start | bytes 4194304 | tf_op jit(solution)/shard_map/all_to_all | solution.py:27
  145.8 67.7 %all-to-all-done = f32[32,16,1024]{2,1,0:T(8,128)S(1)} async-done(((f32[32,16,1024]{2,1,0:T(8,128)}), f32[32,16,1024]{2,1,0:T(8,128)S(1)}, u32[]{:S(2)}, u32[]{:S(2)}) %all-to-all-start) | async-done | bytes 2097184 | tf_op jit(solution)/shard_map/all_to_all | solution.py:27
  214.7 1.6 copy.15
  217.4 2.5 copy.13
  220.0 1.5 fusion.2
  222.5 11.7 %cholesky.320 = f32[128,128]{1,0:T(8,128)S(1)} custom-call(f32[128,128]{1,0:T(8,128)S(1)} %cholesky.460), custom_call_target="Cholesky" | custom-call | tf_op jit(solution)/shard_map/jit(cholesky)/cholesky | solution.py:89
  234.3 9.8 %custom-call.44 = f32[1,128,128]{1,2,0:T(8,128)S(1)} custom-call(f32[1,128,128]{2,1,0:T(8,128)S(1)} %get-tuple-element.86), custom_call_target="InvertDiagBlocksLowerTriangular" | custom-call | tf_op jit(solution)/shard_map/jit(cholesky)/cholesky | solution.py:89
  246.7 11.7 %cholesky.339 = f32[128,128]{1,0:T(8,128)S(1)} custom-call(f32[128,128]{1,0:T(8,128)S(1)} %cholesky.464), custom_call_target="Cholesky" | custom-call | tf_op jit(solution)/shard_map/jit(cholesky)/cholesky | solution.py:89
  258.5 10.2 %custom-call.45 = f32[1,128,128]{1,2,0:T(8,128)S(1)} custom-call(f32[1,128,128]{2,1,0:T(8,128)S(1)} %get-tuple-element.83), custom_call_target="InvertDiagBlocksLowerTriangular" | custom-call | tf_op jit(solution)/shard_map/jit(cholesky)/cholesky | solution.py:89
  270.2 11.7 %cholesky.360 = f32[128,128]{1,0:T(8,128)S(1)} custom-call(f32[128,128]{1,0:T(8,128)S(1)} %cholesky.469), custom_call_target="Cholesky" | custom-call | tf_op jit(solution)/shard_map/jit(cholesky)/cholesky | solution.py:89
  282.0 9.8 %custom-call.46 = f32[1,128,128]{1,2,0:T(8,128)S(1)} custom-call(f32[1,128,128]{2,1,0:T(8,128)S(1)} %get-tuple-element.80), custom_call_target="InvertDiagBlocksLowerTriangular" | custom-call | tf_op jit(solution)/shard_map/jit(cholesky)/cholesky | solution.py:89
  293.3 11.9 %cholesky.377 = f32[128,128]{1,0:T(8,128)S(1)} custom-call(f32[128,128]{1,0:T(8,128)S(1)} %convolution_subtract_fusion.7), custom_call_target="Cholesky" | custom-call | tf_op jit(solution)/shard_map/jit(cholesky)/cholesky | solution.py:89
  309.6 1.4 select_select_fusion.1
  311.0 7.6 %while.10 = (s32[]{:T(128)}, f32[512,512]{1,0:T(8,128)S(1)}, s32[4,2]{0,1:T(2,128)S(1)}, f32[4,128,128]{2,1,0:T(8,128)S(1)}, s32[]{:T(128)}) while((s32[]{:T(128)}, f32[512,512]{1,0:T(8,128)S(1)}, s32[4,2]{0,1:T(2,128)S(1)}, f32[4,128,128]{2,1,0:T(8,128)S(1)}, s32[]{:T(128)}) %tuple.67), condition=%wide.while_cond.1.clone, body=%wide.while_body.1.clone.sunk | while | flops 2 | bytes 131189 | solution.py:51
  311.6 1.3 bitcast_dynamic-update-slice_fusion.5
  319.4 40.2 %custom-call.53 = f32[4,128,128]{1,2,0:T(8,128)S(1)} custom-call(f32[4,128,128]{2,1,0:T(8,128)} %copy-done.11), custom_call_target="InvertDiagBlocksLowerTriangular" | custom-call | tf_op jit(solution)/shard_map/triangular_solve/custom-call.12 | solution.py:51
  359.6 8.1 %copy.16 = f32[8,8,32,1024]{3,2,1,0:T(8,128)S(1)} copy(f32[8,8,32,1024]{3,1,2,0:T(8,128)} %bitcast.180) | data formatting | bytes 16777216
  367.7 1.5 bitcast_reduce_fusion
  372.8 1.4 convolution_subtract_fusion.26
  374.2 23.6 %psum.14 = f32[16,512]{1,0:T(8,128)S(1)} all-reduce(f32[16,512]{1,0:T(8,128)S(1)} %convolution_subtract_fusion.26), channel_id=1, replica_groups=mesh['outer'=8,'inner_0'=4,'inner_1'=8] {'outer'}, use_global_device_ids=true, to_apply=%region_13.15 | all-reduce | flops 8192 | bytes 65536 | tf_op jit(solution)/shard_map/psum | solution.py:93
  399.0 5.5 all-to-all-start.1
  404.9 2.4 convolution_subtract_fusion.5
  407.3 22.8 %all-to-all-done.1 = f32[32,16,512]{2,1,0:T(8,128)S(1)} async-done(((f32[32,16,512]{2,1,0:T(8,128)}), f32[32,16,512]{2,1,0:T(8,128)S(1)}, u32[]{:S(2)}, u32[]{:S(2)}) %all-to-all-start.1) | async-done | bytes 1048608 | tf_op jit(solution)/shard_map/all_to_all | solution.py:27
  430.2 1.3 copy.14
  431.5 1.4 fusion.1
  433.9 11.7 %cholesky.392 = f32[128,128]{1,0:T(8,128)S(1)} custom-call(f32[128,128]{1,0:T(8,128)S(1)} %cholesky.473), custom_call_target="Cholesky" | custom-call | tf_op jit(solution)/shard_map/jit(cholesky)/cholesky | solution.py:98
  446.2 9.8 %custom-call.47 = f32[1,128,128]{1,2,0:T(8,128)S(1)} custom-call(f32[1,128,128]{2,1,0:T(8,128)S(1)} %get-tuple-element.76), custom_call_target="InvertDiagBlocksLowerTriangular" | custom-call | tf_op jit(solution)/shard_map/jit(cholesky)/cholesky | solution.py:98
  459.4 11.7 %cholesky.411 = f32[128,128]{1,0:T(8,128)S(1)} custom-call(f32[128,128]{1,0:T(8,128)S(1)} %cholesky.477), custom_call_target="Cholesky" | custom-call | tf_op jit(solution)/shard_map/jit(cholesky)/cholesky | solution.py:98
  471.8 10.0 %custom-call.48 = f32[1,128,128]{1,2,0:T(8,128)S(1)} custom-call(f32[1,128,128]{2,1,0:T(8,128)S(1)} %get-tuple-element.73), custom_call_target="InvertDiagBlocksLowerTriangular" | custom-call | tf_op jit(solution)/shard_map/jit(cholesky)/cholesky | solution.py:98
  484.9 13.2 %cholesky.432 = f32[128,128]{1,0:T(8,128)} custom-call(f32[128,128]{1,0:T(8,128)} %cholesky.482), custom_call_target="Cholesky" | custom-call | tf_op jit(solution)/shard_map/jit(cholesky)/cholesky | solution.py:98
  498.0 1.5 select_reduce_fusion.1
  500.2 11.3 %custom-call.49 = f32[1,128,128]{1,2,0:T(8,128)} custom-call(f32[1,128,128]{2,1,0:T(8,128)} %get-tuple-element.70), custom_call_target="InvertDiagBlocksLowerTriangular" | custom-call | tf_op jit(solution)/shard_map/jit(cholesky)/cholesky | solution.py:98
  513.7 11.9 %cholesky.449 = f32[128,128]{1,0:T(8,128)S(1)} custom-call(f32[128,128]{1,0:T(8,128)S(1)} %convolution_subtract_fusion.6), custom_call_target="Cholesky" | custom-call | tf_op jit(solution)/shard_map/jit(cholesky)/cholesky | solution.py:98
  530.0 11.5 %while.9 = (s32[]{:T(128)}, f32[512,512]{1,0:T(8,128)}, s32[4,2]{0,1:T(2,128)S(1)}, f32[4,128,128]{2,1,0:T(8,128)S(1)}, s32[]{:T(128)}) while((s32[]{:T(128)}, f32[512,512]{1,0:T(8,128)}, s32[4,2]{0,1:T(2,128)S(1)}, f32[4,128,128]{2,1,0:T(8,128)S(1)}, s32[]{:T(128)}) %tuple.81), condition=%wide.while_cond.1, body=%wide.while_body.1.sunk | while | flops 2 | bytes 131189 | solution.py:51
  530.6 2.3 bitcast_dynamic-update-slice_fusion.4
  533.5 2.3 bitcast_dynamic-update-slice_fusion.4
  536.4 2.3 bitcast_dynamic-update-slice_fusion.4
  539.3 2.2 bitcast_dynamic-update-slice_fusion.4
  541.5 39.3 %custom-call.51 = f32[4,128,128]{1,2,0:T(8,128)S(1)} custom-call(f32[4,128,128]{2,1,0:T(8,128)S(1)} %get-tuple-element.42), custom_call_target="InvertDiagBlocksLowerTriangular" | custom-call | tf_op jit(solution)/shard_map/triangular_solve/custom-call.12 | solution.py:51
  584.6 1.3 convolution_subtract_fusion.23
  (152 shorter events, 58.4 us)
Async XLA Ops:
  8.0 84.0 %reduce-scatter.3.cloned.1.call-start = ((), (), s32[]{:S(2)}) async-start(), calls=%async_computation.4 | async-start | bytes 5242880 | tf_op jit(solution)/shard_map/reduce_scatter | solution.py:21
  39.9 94.2 %reduce-scatter.5.cloned.1.call-start = ((), (), s32[]{:S(2)}) async-start(), calls=%async_computation.5 | async-start | bytes 1179648 | tf_op jit(solution)/shard_map/reduce_scatter | solution.py:21
  92.0 267.5 %all-gather.3.cloned.1.call-start = ((), (), s32[]{:S(2)}) async-start(), calls=%async_computation.7 | async-start | bytes 8650752 | tf_op jit(solution)/shard_map/all_gather | solution.py:16
  136.5 77.0 %all-to-all-start = ((f32[32,16,1024]{2,1,0:T(8,128)}), f32[32,16,1024]{2,1,0:T(8,128)S(1)}, u32[]{:S(2)}, u32[]{:S(2)}) async-start(f32[32,16,1024]{2,1,0:T(8,128)} %broadcast_in_dim.36), calls=%async_computation.2 | async-start | bytes 4194304 | tf_op jit(solution)/shard_map/all_to_all | solution.py:27
  221.4 1.1 copy-start.4
  308.2 1.4 copy-start.2
  318.7 0.7 copy-start.11
  319.4 52.9 %copy-start = (f32[512,512]{1,0:T(8,128)}, f32[512,512]{1,0:T(8,128)S(1)}, u32[]{:S(2)}) copy-start(f32[512,512]{1,0:T(8,128)S(1)} %get-tuple-element.192) | copy-start | bytes 3145732
  369.2 3.4 copy-start.6
  372.8 26.2 %copy-start.10 = (f32[128,80]{0,1:T(8,128)}, f32[128,80]{0,1:T(8,128)S(1)}, u32[]{:S(2)}) copy-start(f32[128,80]{0,1:T(8,128)S(1)} %fusion.129) | copy-start | bytes 122884
  399.0 31.1 %all-to-all-start.1 = ((f32[32,16,512]{2,1,0:T(8,128)}), f32[32,16,512]{2,1,0:T(8,128)S(1)}, u32[]{:S(2)}, u32[]{:S(2)}) async-start(f32[32,16,512]{2,1,0:T(8,128)} %broadcast_in_dim.37), calls=%async_computation.3 | async-start | bytes 2097152 | tf_op jit(solution)/shard_map/all_to_all | solution.py:27
  404.5 176.4 %all-reduce.3.cloned.1.call-start = ((), (), s32[]{:S(2)}) async-start(), calls=%async_computation.6 | async-start | bytes 262144 | tf_op jit(solution)/shard_map/psum | solution.py:93
  432.9 1.0 copy-start.3
  458.7 0.7 copy-start.9
  530.0 60.5 %copy-start.7 = (f32[1024,64]{0,1:T(8,128)S(1)}, f32[1024,64]{0,1:T(8,128)}, u32[]{:S(2)}) copy-start(f32[1024,64]{0,1:T(8,128)} %copy-done.6) | copy-start | bytes 786436
  582.9 8.9 %copy-start.1 = (f32[512,512]{1,0:T(8,128)S(1)}, f32[512,512]{1,0:T(8,128)}, u32[]{:S(2)}) copy-start(f32[512,512]{1,0:T(8,128)} %copy-done) | copy-start | bytes 3145732
  590.5 5.0 copy-start.8
  590.5 4.5 copy-start.5
Sparse Core Ops, SparseCore 0:
  40.0 51.9 reduce-scatter.2
  94.7 39.2 reduce-scatter.4
  408.3 63.7 all-reduce.2
Sparse Core Ops, SparseCore 1:
  95.4 131.9 all-gather.2
where the time goes:
time: 613 us; the launch traced here: 604 us
  other arithmetic  274 us (45%)
  waiting for transfers between devices  183 us (30%)
  matrix products  43.8 us (7%)
  local copies, waits for them, and re-layouts  43.4 us (7%)
  blocking collectives  23.6 us (4%)
  between operations  21.1 us (3%)
  starting transfers between devices  14.5 us (2%)
    reduce_scatter x2, waiting for transfers between devices, summed_rows(): total = lax.psum_scatter(total, axis, scatter_dimension=0, tiled=True)  92.6 us
    all_to_all x2, waiting for transfers between devices, sent_to_all(): return lax.all_to_all(copies, axis, split_axis=0, concat_axis=0, tiled=True)  90.5 us
    another operation x15, other arithmetic, shards(): root_coef = factor_solve(jnp.linalg.cholesky(precision_root), reduced_total)  83.8 us
    another operation x6, other arithmetic, factor_solve(): lax.linalg.triangular_solve(factor, first, left_side=True, lower=True, tr...  82 us
    another operation x14, other arithmetic, shards(): knot_factor = jnp.linalg.cholesky(knot_block)  79 us
    psum x1, blocking collectives, shards(): schur_total, reduced_total = lax.psum((schur_part, reduced), 'outer')  23.6 us
    another operation x27, local copies, waits for them, and re-layouts, factor_solve(): lax.linalg.triangular_solve(factor, first, left_side=True, lower=True, tr...  19.1 us
    unnamed x27, local copies, waits for them, and re-layouts  14 us
  transfers between devices with their start and end apart: 6, of which 4 were waited for; matrix products, arithmetic and copies ran while one was open for 49% of the time, Pallas kernels for 0%

commit v1 on v0

v1 whole, which is shorter than its diff:
```python
import functools

import jax
import jax.numpy as jnp
from jax import lax
from jax.experimental import pallas as pl
from jax.experimental.pallas import tpu as pltpu
from jax.sharding import Mesh
from jax.sharding import PartitionSpec as P

M = 512
R = 512
K = 1024
F = 64
RANGE = 8
B = 128
PIVOTS = 8
NB = M // B
OUTER_INNER = ("outer", "inner_0", "inner_1")
PAIRS = [(i, j) for i in range(NB) for j in range(i, NB)]
TRI = {pair: at for at, pair in enumerate(PAIRS)}
A_ROWS = len(PAIRS) * B
X_ROWS = (NB * NB + NB) * B
RED_ROWS = R // 2


def dot(left, right, left_dim=1):
    return lax.dot_general(
        left,
        right,
        (((left_dim,), (0,)), ((), ())),
        precision=lax.Precision.HIGHEST,
        preferred_element_type=jnp.float32,
    )


def swept(block, n):
    def at(values, q, k):
        return values[(min(q, k), max(q, k))]

    for p in range(n):
        inverse = 1.0 / block[(p, p)]
        scaled = {q: at(block, q, p) * inverse for q in range(n) if q != p}
        new = {}
        for q in range(n):
            for k in range(q, n):
                if q == p and k == p:
                    new[(q, k)] = -inverse
                elif q == p:
                    new[(q, k)] = scaled[k]
                elif k == p:
                    new[(q, k)] = scaled[q]
                else:
                    new[(q, k)] = block[(q, k)] - scaled[q] * at(block, p, k)
        block = new
    return block


def panel(x):
    n = x.shape[0]
    b = PIVOTS
    lane = lax.broadcasted_iota(jnp.int32, (b, n), 1)
    sub = lax.broadcasted_iota(jnp.int32, (b, n), 0)
    columns = [jnp.broadcast_to(x[:, k : k + 1], (n, n)) for k in range(b)]
    block = {
        (q, k): jnp.broadcast_to(columns[k][q : q + 1, :], (b, n))
        for q in range(b)
        for k in range(q, b)
    }
    minus_inverse = swept(block, b)
    top = jnp.where(lane < b, jnp.where(lane == sub, -1.0, 0.0), x[0:b, :])
    rows = [jnp.broadcast_to(top[k : k + 1, :], (b, n)) for k in range(b)]
    minus_new = []
    for q in range(b):
        total = None
        for k in range(b):
            term = minus_inverse[(min(q, k), max(q, k))] * rows[k]
            total = term if total is None else total + term
        minus_new.append(total)
    tiles = []
    for t in range(1, n // b):
        tile = jnp.where(lane < b, 0.0, x[t * b : (t + 1) * b, :])
        for k in range(b):
            tile = tile + columns[k][t * b : (t + 1) * b, :] * minus_new[k]
        tiles.append(tile)
    first = minus_new[0]
    for q in range(1, b):
        first = jnp.where(sub == q, minus_new[q], first)
    tiles.append(-first)
    return pltpu.roll(jnp.concatenate(tiles, axis=0), n - b, 1)


def minus_inverse_of(x):
    return lax.fori_loop(0, x.shape[0] // PIVOTS, lambda _, held: panel(held), x)


def sweep_block(x_ref, new_ref, k):
    at = slice(k * B, (k + 1) * B)
    minus = minus_inverse_of(x_ref[at, at])
    new_ref[...] = -dot(minus, x_ref[at, :])
    new_ref[:, at] = minus
    new = new_ref[...]
    for i in range(NB):
        if i != k:
            rows = slice(i * B, (i + 1) * B)
            left = x_ref[at, rows]
            x_ref[rows, at] = jnp.zeros((B, B), jnp.float32)
            x_ref[rows, :] = x_ref[rows, :] - dot(left, new, 0)
    x_ref[at, :] = new


def fill_symmetric(x_ref, packed_ref):
    diagonal = lax.broadcasted_iota(jnp.int32, (B, B), 0) == lax.broadcasted_iota(
        jnp.int32, (B, B), 1
    )
    eye = jnp.where(diagonal, 1.0, 0.0)
    for (i, j), block in TRI.items():
        value = packed_ref[block * B : (block + 1) * B, :]
        ri, rj = slice(i * B, (i + 1) * B), slice(j * B, (j + 1) * B)
        if i == j:
            x_ref[ri, ri] = value + eye
        else:
            x_ref[ri, rj] = value
            x_ref[rj, ri] = value.T


def kernel(
    no,
    ny,
    nz,
    basis_ref,
    fields_ref,
    positions_ref,
    nugget_ref,
    mean_ref,
    root_ref,
    solved,
    padded,
    local_a,
    local_x,
    local_g,
    ya_in,
    yx_in,
    yg_in,
    ya,
    yx,
    yg,
    za_in,
    zx_in,
    zg_in,
    all_a,
    all_x,
    mine_g,
    knot,
    new_rows,
    weights,
    correction,
    outer_in,
    all_p,
    packed_p,
    root,
    sy,
    ry,
    sz,
    rz,
    gsz,
    grz,
    gsy,
    gry,
    so,
    ro,
):
    o = lax.axis_index("outer")
    y = lax.axis_index("inner_0")
    z = lax.axis_index("inner_1")
    me = y * nz + z
    inner = ny * nz

    def y_peer(k):
        return {"inner_0": lax.rem(y + k, ny)}

    def z_peer(k):
        return {"inner_1": lax.rem(z + k, nz)}

    def o_peer(k):
        return {"outer": lax.rem(o + k, no)}

    peers = (
        [y_peer(k) for k in range(1, ny)]
        + [z_peer(k) for k in range(1, nz)]
        + [o_peer(k) for k in range(1, no)]
    )
    barrier = pltpu.get_barrier_semaphore()
    for peer in peers:
        pl.semaphore_signal(barrier, inc=1, device_id=peer, device_id_type=pl.DeviceIdType.MESH)

    sent = []

    def send(src, dst, send_sem, recv_sem, peer):
        copy = pltpu.make_async_remote_copy(
            src_ref=src,
            dst_ref=dst,
            send_sem=send_sem,
            recv_sem=recv_sem,
            device_id=peer,
            device_id_type=pl.DeviceIdType.MESH,
        )
        copy.start()
        sent.append(copy)
        return copy

    def span(index, rows):
        return pl.ds(pl.multiple_of(index * rows, 8), rows)

    def sum_y(part, local, landing):
        rows = local.shape[0] // ny
        return [
            send(
                local.at[span(lax.rem(y + k, ny), rows)],
                landing.at[k - 1],
                sy.at[part, k - 1],
                ry.at[part, k - 1],
                y_peer(k),
            )
            for k in range(1, ny)
        ]

    def sum_z(part, held, landing):
        rows = held.shape[0] // nz
        return [
            send(
                held.at[span(lax.rem(z + k, nz), rows)],
                landing.at[k - 1],
                sz.at[part, k - 1],
                rz.at[part, k - 1],
                z_peer(k),
            )
            for k in range(1, nz)
        ]

    def gather_z(part, full):
        rows = full.shape[0] // inner
        own = full.at[span(me, rows)]
        return [
            send(own, own, gsz.at[part, k - 1], grz.at[part, k - 1], z_peer(k))
            for k in range(1, nz)
        ]

    def gather_y(part, full):
        rows = full.shape[0] // ny
        own = full.at[span(y, rows)]
        return [
            send(own, own, gsy.at[part, k - 1], gry.at[part, k - 1], y_peer(k))
            for k in range(1, ny)
        ]

    def arrived(copies):
        for copy in copies:
            copy.wait_recv()

    def summed(landing, own):
        total = own
        for k in range(landing.shape[0]):
            total = total + landing[k]
        return total

    def own_rows(ref, index, parts):
        return ref[span(index, ref.shape[0] // parts), :]

    position = jnp.broadcast_to(positions_ref[...].astype(jnp.float32), (B, B))
    diagonal = lax.broadcasted_iota(jnp.int32, (B, B), 0) == lax.broadcasted_iota(
        jnp.int32, (B, B), 1
    )
    covariance = jnp.exp(-jnp.abs(position - position.T) / RANGE) + jnp.where(
        diagonal, jnp.broadcast_to(nugget_ref[...], (B, B)), 0.0
    )
    minus = minus_inverse_of(covariance)
    solved[...] = -dot(minus, basis_ref[...])

    for i in range(NB):
        row = dot(basis_ref[:, i * B : (i + 1) * B], solved[:, i * B : M], 0)
        for j in range(i, NB):
            at = TRI[(i, j)] * B
            local_a[at : at + B, :] = row[:, (j - i) * B : (j - i + 1) * B]
    pl.semaphore_wait(barrier, len(peers))
    a_y = sum_y(0, local_a, ya_in)
    for i in range(NB):
        row = dot(basis_ref[:, i * B : (i + 1) * B], solved[:, M:], 0)
        for j in range(NB):
            at = (i * NB + j) * B
            local_x[at : at + B, :] = row[:, j * B : (j + 1) * B]
    padded[...] = jnp.zeros_like(padded)
    padded[:, 0:F] = fields_ref[...]
    left_fields = -dot(minus, padded[...])
    right_fields = pltpu.roll(left_fields, F, 1)
    for i in range(NB):
        at = (NB * NB + i) * B
        local_x[at : at + B, :] = dot(
            basis_ref[:, i * B : (i + 1) * B], left_fields, 0
        ) + dot(basis_ref[:, M + i * B : M + (i + 1) * B], right_fields, 0)
    x_y = sum_y(1, local_x, yx_in)
    arrived(a_y)
    ya[...] = summed(ya_in, own_rows(local_a, y, ny))
    a_z = sum_z(0, ya, za_in)
    for i in range(NB):
        row = dot(
            basis_ref[:, M + i * B : M + (i + 1) * B], solved[:, M + i * B :], 0
        )
        for j in range(i, NB):
            at = TRI[(i, j)] * B
            local_g[at : at + B, :] = row[:, (j - i) * B : (j - i + 1) * B]
    arrived(a_z)
    all_a[span(me, A_ROWS // inner), :] = summed(za_in, own_rows(ya, z, nz))
    a_gz = gather_z(0, all_a)
    arrived(a_gz)
    a_gy = gather_y(0, all_a)
    arrived(x_y)
    yx[...] = summed(yx_in, own_rows(local_x, y, ny))
    x_z = sum_z(1, yx, zx_in)
    g_y = sum_y(2, local_g, yg_in)
    arrived(a_gy)

    fill_symmetric(knot, all_a)
    sweep_block(knot, new_rows, 0)
    arrived(x_z)
    all_x[span(me, X_ROWS // inner), :] = summed(zx_in, own_rows(yx, z, nz))
    x_gz = gather_z(1, all_x)
    sweep_block(knot, new_rows, 1)
    arrived(x_gz)
    x_gy = gather_y(1, all_x)
    arrived(g_y)
    yg[...] = summed(yg_in, own_rows(local_g, y, ny))
    g_z = sum_z(2, yg, zg_in)
    sweep_block(knot, new_rows, 2)
    sweep_block(knot, new_rows, 3)
    arrived(g_z)
    mine_g[...] = summed(zg_in, own_rows(yg, z, nz))
    arrived(x_gy)

    for i in range(NB):
        rows = slice(i * B, (i + 1) * B)
        total = None
        for k in range(NB):
            right = jnp.concatenate(
                [all_x[(k * NB + j) * B : (k * NB + j + 1) * B, :] for j in range(NB)]
                + [all_x[(NB * NB + k) * B : (NB * NB + k + 1) * B, :]],
                axis=1,
            )
            term = dot(knot[rows, k * B : (k + 1) * B], right)
            total = term if total is None else total + term
        weights[rows, :] = -total
    reduced = []
    for i in range(NB):
        total = None
        for k in range(NB):
            left = all_x[(k * NB + i) * B : (k * NB + i + 1) * B, :]
            term = dot(left, weights[k * B : (k + 1) * B, i * B :], 0)
            total = term if total is None else total + term
        for j in range(i, NB):
            at = TRI[(i, j)] * B
            correction[at : at + B, :] = total[:, (j - i) * B : (j - i + 1) * B]
        root_rhs = pltpu.roll(all_x[(NB * NB + i) * B : (NB * NB + i + 1) * B, :], F, 1)
        reduced.append(root_rhs - total[:, (NB - i) * B :])
    lane = lax.broadcasted_iota(jnp.int32, (B, B), 1)
    for i in range(NB // 2):
        at = A_ROWS + i * B
        correction[at : at + B, :] = jnp.where(
            lane < F, reduced[i], pltpu.roll(reduced[i + NB // 2], F, 1)
        )
    a_share, r_share = A_ROWS // inner, RED_ROWS // inner
    share = a_share + r_share
    outer_in[o, 0:a_share, :] = mine_g[...] - correction[span(me, a_share), :]
    outer_in[o, a_share:share, :] = correction[
        pl.ds(pl.multiple_of(A_ROWS + me * r_share, 8), r_share), :
    ]
    outer = [
        send(outer_in.at[o], outer_in.at[o], so.at[k - 1], ro.at[k - 1], o_peer(k))
        for k in range(1, no)
    ]
    arrived(outer)
    total = outer_in[0]
    for k in range(1, no):
        total = total + outer_in[k]
    all_p[span(me, share), :] = total
    p_gz = gather_z(2, all_p)
    arrived(p_gz)
    p_gy = gather_y(2, all_p)
    arrived(p_gy)
    for d in range(inner):
        packed_p[d * a_share : (d + 1) * a_share, :] = all_p[d * share : d * share + a_share, :]
        at = A_ROWS + d * r_share
        packed_p[at : at + r_share, :] = all_p[d * share + a_share : (d + 1) * share, :]

    fill_symmetric(root, packed_p)
    for k in range(NB):
        sweep_block(root, new_rows, k)
    half = packed_p[A_ROWS:, :]
    root_coef = -dot(root[...], jnp.concatenate([half, pltpu.roll(half, F, 1)], axis=0))
    root_ref[...] = root_coef[:, 0:F]
    region_coef = weights[:, M:] - dot(weights[:, 0:M], root_coef)
    mean = dot(basis_ref[:, 0:M], region_coef) + dot(basis_ref[:, M:], root_coef)
    mean_ref[...] = mean[:, 0:F]
    for copy in sent:
        copy.wait_send()


def shards(basis, fields, positions, nugget):
    no, ny, nz = (lax.axis_size(axis) for axis in OUTER_INNER)
    inner = ny * nz
    f32 = jnp.float32

    def landing(parts, rows):
        return pltpu.VMEM((parts, rows, B), f32)

    def flat(rows):
        return pltpu.VMEM((rows, B), f32)

    share = (A_ROWS + RED_ROWS) // inner
    dma = pltpu.SemaphoreType.DMA
    scratch = (
        [pltpu.VMEM((B, K), f32), flat(B), flat(A_ROWS), flat(X_ROWS), flat(A_ROWS)]
        + [landing(ny - 1, rows // ny) for rows in (A_ROWS, X_ROWS, A_ROWS)]
        + [flat(rows // ny) for rows in (A_ROWS, X_ROWS, A_ROWS)]
        + [landing(nz - 1, rows // inner) for rows in (A_ROWS, X_ROWS, A_ROWS)]
        + [flat(A_ROWS), flat(X_ROWS), flat(A_ROWS // inner)]
        + [pltpu.VMEM((M, M), f32), pltpu.VMEM((B, M), f32), pltpu.VMEM((M, M + B), f32)]
        + [flat(A_ROWS + RED_ROWS), landing(no, share), flat(A_ROWS + RED_ROWS)]
        + [flat(A_ROWS + RED_ROWS), pltpu.VMEM((R, R), f32)]
        + [dma((3, ny - 1)), dma((3, ny - 1)), dma((3, nz - 1)), dma((3, nz - 1))]
        + [dma((3, nz - 1)), dma((3, nz - 1)), dma((3, ny - 1)), dma((3, ny - 1))]
        + [dma((no - 1,)), dma((no - 1,))]
    )
    return pl.pallas_call(
        functools.partial(kernel, no, ny, nz),
        out_shape=(
            jax.ShapeDtypeStruct((B, F), f32),
            jax.ShapeDtypeStruct((R, F), f32),
        ),
        in_specs=[pl.BlockSpec(memory_space=pltpu.VMEM)] * 4,
        out_specs=(pl.BlockSpec(memory_space=pltpu.VMEM),) * 2,
        scratch_shapes=scratch,
        compiler_params=pltpu.CompilerParams(
            collective_id=0, has_side_effects=True, vmem_limit_bytes=48 * 1024 * 1024
        ),
    )(basis, fields, positions.reshape(1, B), nugget.reshape(1, B))


def solution(mesh):
    split = Mesh(mesh.devices.reshape(mesh.shape["outer"], 4, 8), ("outer", "inner_0", "inner_1"))
    in_specs = (P(OUTER_INNER, None), P(OUTER_INNER, None), P(OUTER_INNER), P(OUTER_INNER))
    out_specs = (P(OUTER_INNER, None), P())
    return jax.shard_map(
        shards, mesh=split, in_specs=in_specs, out_specs=out_specs, check_vma=False
    )
```

time: 613 us -> 147 us (0.24)
  the two profiles are of different devices: /device:TPU:32 before, /device:TPU:1 now
where the time goes in v1:
time: 147 us; the launch traced here: 146 us
  Pallas kernels  142 us (97%)
  local copies, waits for them, and re-layouts  3.37 us (2%)
    pallas_call x1, Pallas kernels, shards(): pl.pallas_call(functools.partial(kernel, no, ny, nz), out_shape=(jax.Shap...  142 us

profile of v1, /device:TPU:1, one launch (start us, length us, event | category | flops | bytes accessed | tf_op | source)
XLA Modules:
  0.0 145.7 jit_solution(1273960048475762260)
XLA Ops:
  0.6 0.0 copy-start.1
  0.6 0.0 copy-start.2
  0.7 0.9 copy.6.fields_ref
  1.5 0.0 copy-done.1
  1.5 0.0 copy-done.2
  1.5 0.0 copy-start
  1.5 1.0 copy-done
  2.6 141.6 %shard_map.59 = (f32[128,64]{1,0:T(8,128)S(1)}, f32[512,64]{1,0:T(8,128)S(1)}) custom-call(f32[128,1024]{1,0:T(8,128)S(1)} %copy-done, f32[128,64]{1,0:T(8,128)S(1)} %copy.6.fields_ref, s32[1,128]{1,0:T(1,128)S(1)} %bitcast.2, f32[1,128]{1,0:T(1,128)S(1)} %bitcast.3), custom_call_target="tpu_custom_call" | custom-call | tf_op jit(solution)/shard_map/pallas_call | solution.py:433
  144.2 0.7 copy.7
  144.9 0.8 copy.8
Async XLA Ops:
  0.6 0.9 copy-start.1
  0.6 0.9 copy-start.2
  1.5 1.0 copy-start
